TPU v7x, 256 devices: a whole 4x4x8 slice. The times are simulated.
256 devices in a mesh: slab: 128 (over y, z, x), blk: 2 (over core).
Axes of the slice: x: 4, y: 4, z: 8, core: 2. Of those that a mesh axis runs over, the one named last changes fastest.
Arguments:
- slip_rate: float32 [262144], P('slab'), may hold values from 0.1 to 3
- log_state: float32 [262144], P('slab'), may hold values from -1 to 1
- friction_a: float32 [262144], P('slab'), may hold values from 0.2 to 1
- friction_b: float32 [262144], P('slab'), may hold values from 0.2 to 1
- normal_stress: float32 [262144], P('slab'), may hold values from 2 to 4
- leak_rate: float32 [262144], P('slab'), may hold values from 0.5 to 2
- corner: int32 [3, 262144], P(None, 'slab'), may hold values from 0 to 1022, as said below
- fraction: float32 [3, 262144], P(None, 'slab'), may hold values from 0 to 1
- near_blocks: bfloat16 [512, 3, 512, 512], P(('slab', 'blk')), may hold values from -0.15625 to 0.15625
- row_basis: bfloat16 [24, 262144], P(None, 'slab'), may hold values from -1.25 to 1.25
- col_basis: bfloat16 [24, 262144], P(None, 'slab'), may hold values from -0.25 to 0.25
- far_row: int32 [262144], P(('slab', 'blk')), may hold values from 0 to 3
- far_col: int32 [262144], P(('slab', 'blk')), may hold values from 0 to 511, as said below
- far_rank: int32 [262144], P(('slab', 'blk')), may hold values from 0 to 24, as said below
- far_coupling: bfloat16 [24, 24, 262144], P(None, None, ('slab', 'blk')), may hold values from -0.078125 to 0.078125
- pressure: float32 [256, 512, 1024], P('slab', 'blk'), may hold values from -1 to 1
- region: int32 [256, 512, 1024], P('slab', 'blk'), may hold values from 0 to 15
- perm_table: float32 [16], replicated, may hold values from 0.05 to 1
Outputs:
- slip_accel: float32 [262144], P('slab')
- state_rate: float32 [262144], P('slab')
- pressure_rate: float32 [256, 512, 1024], P('slab', 'blk')
Inputs may be any that keep to these rules, and one draw needn't show every extreme that they name: corner[0, f] equals 2 * (f // 2048), the first plane of the slab that holds cell f; corner[1, f] is at most 510 and corner[2, f] at most 1022. far_col[s] differs by 2 or more (cyclically over 512 clusters) from the slot's row cluster 4 * (s // 2048) + far_row[s]. `far_rank`: slots with rank 0 are empty; the live slots of a device come first, and some device has all 1024 slots live.
All inputs are finite; a program needn't handle non-finite values.
Results may differ from a plain program's by a relative error of at most 0.0022.
Values may be sent and summed in bfloat16 or wider, within the bound.
A program may use at most 64 MiB of HBM per device.

v0:
```python
import functools

import jax
import jax.numpy as jnp
from jax import lax
from jax.experimental import pallas as pl
from jax.experimental.pallas import tpu as pltpu
from jax.sharding import Mesh
from jax.sharding import PartitionSpec as P

SLAB = ("slab_0", "slab_1", "slab_2")
SLAB_BLK = ("slab_0", "slab_1", "slab_2", "blk")
MESH = pl.DeviceIdType.MESH

PARTS = 4
F_TILE = 256
HALO = 8
FAR = 1e30


def lanes_row(ref, first, count):
    return jnp.concatenate([ref[first + q : first + q + 1, :] for q in range(count)], axis=1)


def store_rows(ref, first, row):
    for q in range(row.shape[1] // 128):
        ref[first + q : first + q + 1, :] = row[:, 128 * q : 128 * (q + 1)]


def inverse(x):
    return pl.reciprocal(x, approx=True)


def kernel(
    sizes,
    slip,
    log_state,
    friction_a,
    friction_b,
    stress,
    leak,
    corner,
    fraction,
    row_basis,
    col_basis,
    far_row,
    far_col,
    far_rank,
    table,
    near_hbm,
    coupling_hbm,
    p_hbm,
    region_hbm,
    rate_hbm,
    accel_out,
    state_out,
    pv,
    rv,
    region,
    acc,
    snd,
    rcv,
    fsnd,
    frcv,
    p_edge,
    r_edge,
    wz,
    wyx,
    p_low,
    near,
    coupling,
    pick,
    gather_x,
    gather,
    slip_edge,
    window,
    flow_row,
    fp_row,
    fp_own,
    fp_other,
    near_own,
    near_other,
    tot_own,
    tot_other,
    block,
    far16,
    load_sem,
    x_send,
    x_recv,
    z_send,
    z_recv,
    y_send,
    y_recv,
    pr_send,
    pr_recv,
    fl_send,
    fl_recv,
    one_send,
    one_recv,
    out_sem,
):
    ny, nz, nx = sizes
    slabs = ny * nz * nx
    planes, width_y, width_z = region.shape
    half = width_y // 2
    rows = half // PARTS
    rank = col_basis.shape[0]
    cells = corner.shape[1]
    yi, zi, xi = (lax.axis_index(name) for name in SLAB)
    bi = lax.axis_index("blk")
    slab = (yi * nz + zi) * nx + xi

    def chip_of(index):
        return (
            lax.div(index, nz * nx),
            lax.rem(lax.div(index, nx), nz),
            lax.rem(index, nx),
            bi,
        )

    above = chip_of(lax.rem(slab + 1, slabs))
    below = chip_of(lax.rem(slab + slabs - 1, slabs))
    other = (yi, zi, xi, 1 - bi)
    x_peers = [(yi, zi, lax.rem(xi + d, nx), bi) for d in range(1, nx)]
    z_peers = [(yi, lax.rem(zi + d, nz), xi, bi) for d in range(1, nz)]
    y_peers = [(lax.rem(yi + d, ny), zi, xi, bi) for d in range(1, ny)]

    barrier = pltpu.get_barrier_semaphore()
    peers = [above, below, other] + x_peers + z_peers + y_peers
    for peer in peers:
        pl.semaphore_signal(barrier, inc=1, device_id=peer, device_id_type=MESH)

    def remote(src, dst, send, recv, device):
        return pltpu.make_async_remote_copy(
            src_ref=src,
            dst_ref=dst,
            send_sem=send,
            recv_sem=recv,
            device_id=device,
            device_id_type=MESH,
        )

    def quarter(plane, part, sem):
        at = pl.ds(part * half, half)
        to = pl.ds(HALO + part * half, half)
        return (
            pltpu.make_async_copy(
                region_hbm.at[plane, at], region.at[plane, at], load_sem.at[sem]
            ),
            pltpu.make_async_copy(p_hbm.at[plane, at], pv.at[plane, to], load_sem.at[sem + 1]),
        )

    first_up, first_down = quarter(1, 0, 0), quarter(0, 1, 2)
    later = quarter(0, 0, 4) + quarter(1, 1, 6)
    load_near = pltpu.make_async_copy(near_hbm, near, load_sem.at[8])
    load_coupling = pltpu.make_async_copy(coupling_hbm, coupling, load_sem.at[9])
    for copy in first_up + first_down + later + (load_near, load_coupling):
        copy.start()

    for c in range(4):
        window[1 + c : 2 + c, :] = lanes_row(slip, 4 * c, 4)
    slip_row = jnp.concatenate([window[1 + c : 2 + c, :] for c in range(4)], axis=1)
    spread = jnp.broadcast_to(slip_row, (8, cells))
    lane = lax.broadcasted_iota(jnp.int32, (8, cells), 1)
    sub = lax.broadcasted_iota(jnp.int32, (8, cells), 0)
    spread = jnp.where(
        (lane >= sub * 512) & (lane < sub * 512 + 512), spread, jnp.float32(0.0)
    ).astype(jnp.bfloat16)
    moments = lax.dot_general(
        spread, col_basis[...], (((1,), (1,)), ((), ())), preferred_element_type=jnp.float32
    )
    gather_x[xi] = jnp.zeros((8, 128), jnp.float32)
    gather_x[xi, :, 0:rank] = moments
    for c in range(16):
        flow_row[:, 128 * c : 128 * (c + 1)] = leak[c : c + 1, :] * slip[c : c + 1, :]

    pl.semaphore_wait(barrier, len(peers))

    x_copies = [
        remote(gather_x.at[xi], gather_x.at[xi], x_send.at[d], x_recv.at[d], peer)
        for d, peer in enumerate(x_peers)
    ]
    for copy in x_copies:
        copy.start()
    slip_up = remote(slip.at[8:16], slip_edge.at[0], one_send.at[0], one_recv.at[0], above)
    slip_down = remote(slip.at[0:8], slip_edge.at[1], one_send.at[1], one_recv.at[1], below)
    slip_up.start()
    slip_down.start()

    def look_up(plane, start, count):
        chosen = region[plane, pl.ds(start, count), :]
        entries = jnp.broadcast_to(table[0:1, :], (count, 128))
        r = jnp.concatenate(
            [
                jnp.take_along_axis(
                    entries,
                    chosen[:, 128 * j : 128 * (j + 1)],
                    axis=1,
                    mode="promise_in_bounds",
                )
                for j in range(width_z // 128)
            ],
            axis=1,
        )
        p = pv[plane, pl.ds(HALO + start, count), :].astype(jnp.bfloat16)
        rv[plane, pl.ds(HALO + start, count), :] = r
        p_low[pl.ds(plane * width_y + start, count), :] = p
        return p, r.astype(jnp.bfloat16)

    pr_copies = []
    for part in range(PARTS):
        for way, plane, offset, device, loads in (
            (0, 1, 0, above, first_up),
            (1, 0, half, below, first_down),
        ):
            if part == 0:
                for copy in loads:
                    copy.wait()
            p, r = look_up(plane, offset + part * rows, rows)
            snd[way, part, 0] = p
            snd[way, part, 1] = r
            copy = remote(
                snd.at[way, part],
                rcv.at[way, part],
                pr_send.at[way, part],
                pr_recv.at[way, part],
                device,
            )
            copy.start()
            pr_copies.append(copy)

    for copy in later:
        copy.wait()

    def rest(step, carry):
        start = pl.multiple_of(step * rows, rows)
        look_up(0, start, rows)
        look_up(1, start + half, rows)
        return carry

    lax.fori_loop(0, PARTS, rest, 0)

    edge = pl.multiple_of(HALO + (1 - bi) * (width_y - 8), 8)
    p_copy = remote(
        pv.at[:, pl.ds(edge, 8), :], p_edge, one_send.at[2], one_recv.at[2], other
    )
    r_copy = remote(
        rv.at[:, pl.ds(edge, 8), :], r_edge, one_send.at[3], one_recv.at[3], other
    )
    p_copy.start()
    r_copy.start()

    for copy in x_copies:
        copy.wait_recv()
    mine = jnp.concatenate([gather_x[i, 0:4, :] for i in range(nx)], axis=0)
    gather[yi, zi] = mine.astype(jnp.bfloat16)
    z_copies = [
        remote(gather.at[yi, zi], gather.at[yi, zi], z_send.at[d], z_recv.at[d], peer)
        for d, peer in enumerate(z_peers)
    ]
    for copy in z_copies:
        copy.start()

    y_start = bi * width_y

    def sample(step, carry):
        at = pl.ds(pl.multiple_of(step * F_TILE, F_TILE), F_TILE)
        z = corner[2:3, at]
        fz = fraction[2:3, at]
        iota = lax.broadcasted_iota(jnp.int32, (width_z, F_TILE), 0)
        weight = jnp.where(
            iota == z, 1.0 - fz, jnp.where(iota == z + 1, fz, jnp.float32(0.0))
        ).astype(jnp.bfloat16)
        wz[:, at] = weight
        along_z = jnp.dot(p_low[...], weight, preferred_element_type=jnp.float32)
        y = corner[1:2, at] - y_start
        fy = fraction[1:2, at]
        fx = fraction[0:1, at]
        flow = flow_row[:, at]
        iota = lax.broadcasted_iota(jnp.int32, (width_y, F_TILE), 0)
        weight_y = jnp.where(iota == y, 1.0 - fy, jnp.where(iota == y + 1, fy, jnp.float32(0.0)))
        low = jnp.sum(along_z[:width_y] * weight_y, axis=0, keepdims=True)
        high = jnp.sum(along_z[width_y:] * weight_y, axis=0, keepdims=True)
        fp_row[:, at] = (1.0 - fx) * low + fx * high
        wyx[0:width_y, at] = (weight_y * ((1.0 - fx) * flow)).astype(jnp.bfloat16)
        wyx[width_y:, at] = (weight_y * (fx * flow)).astype(jnp.bfloat16)
        return carry

    steps = cells // F_TILE
    lax.fori_loop(0, steps // 2, sample, 0)

    for copy in z_copies:
        copy.wait_recv()
    y_copies = [
        remote(gather.at[yi], gather.at[yi], y_send.at[d], y_recv.at[d], peer)
        for d, peer in enumerate(y_peers)
    ]
    for copy in y_copies:
        copy.start()

    has_below = jnp.where(slab > 0, 1.0, 0.0).astype(jnp.float32)
    has_above = jnp.where(slab < slabs - 1, 1.0, 0.0).astype(jnp.float32)
    fl_copies = {}

    def faces(part):
        for way, plane, offset, device, present in (
            (0, 0, 0, below, has_below),
            (1, 1, half, above, has_above),
        ):
            pr_copies[2 * part + way].wait_recv()
            at = pl.ds(HALO + offset + part * rows, rows)
            p_in = rcv[way, part, 0].astype(jnp.float32)
            r_in = rcv[way, part, 1].astype(jnp.float32)
            drop = pv[plane, at, :] - p_in
            flux = drop * (inverse(rv[plane, at, :] + r_in) * -present)
            fsnd[way, part] = flux.astype(jnp.bfloat16)
            copy = remote(
                fsnd.at[way, part],
                frcv.at[way, part],
                fl_send.at[way, part],
                fl_recv.at[way, part],
                device,
            )
            copy.start()
            fl_copies[way, part] = copy

    faces(0)
    lax.fori_loop(steps // 2, steps, sample, 0)
    for c in range(16):
        fp_own[c : c + 1, :] = fp_row[:, 128 * c : 128 * (c + 1)]
    fp_copy = remote(fp_own, fp_other, one_send.at[4], one_recv.at[4], other)
    fp_copy.start()
    faces(1)

    slip_up.wait_recv()
    slip_down.wait_recv()
    window[0:1, :] = has_below * jnp.concatenate(
        [slip_edge[0, 4 + q : 5 + q, :] for q in range(4)], axis=1
    )
    window[5:6, :] = has_above * jnp.concatenate(
        [slip_edge[1, q : 1 + q, :] for q in range(4)], axis=1
    )
    load_near.wait()
    for i in range(2):
        total = jnp.zeros((8, 512), jnp.float32)
        for j in range(3):
            row = window[pl.ds(2 * bi + i + j, 1), :]
            row = jnp.broadcast_to(row, (8, 512)).astype(jnp.bfloat16)
            total = total + lax.dot_general(
                row, near[i, j], (((1,), (1,)), ((), ())), preferred_element_type=jnp.float32
            )
        store_rows(near_own, 4 * i, total[0:1, :])
    near_copy = remote(near_own, near_other, one_send.at[5], one_recv.at[5], other)
    near_copy.start()

    column = lanes_row(far_col, 0, 8)
    pick[...] = jnp.where(
        lax.broadcasted_iota(jnp.int32, pick.shape, 0) == column, 1.0, 0.0
    ).astype(jnp.bfloat16)
    for copy in y_copies:
        copy.wait_recv()
    moments = gather[...].reshape(512, 128)[:, 0:rank]
    picked = lax.dot_general(
        moments, pick[...], (((0,), (0,)), ((), ())), preferred_element_type=jnp.float32
    )
    ranks = lanes_row(far_rank, 0, 8)
    masked = jnp.where(
        lax.broadcasted_iota(jnp.int32, picked.shape, 0) < ranks, picked, jnp.float32(0.0)
    )
    load_coupling.wait()
    for a in range(rank):
        block[a : a + 1, :] = jnp.sum(
            coupling[a].astype(jnp.float32) * masked, axis=0, keepdims=True
        )
    target = lanes_row(far_row, 0, 8)
    lane = lax.broadcasted_iota(jnp.int32, (rank, 128), 1)
    totals = jnp.zeros((rank, 128), jnp.float32)
    for c in range(4):
        share = jnp.sum(
            jnp.where(target == c, block[...], jnp.float32(0.0)), axis=1, keepdims=True
        )
        totals = totals + jnp.where(lane == c, share, jnp.float32(0.0))
    tot_own[...] = totals
    tot_copy = remote(tot_own, tot_other, one_send.at[6], one_recv.at[6], other)
    tot_copy.start()

    def spread_source(step, carry):
        at = pl.ds(pl.multiple_of(step * 256, 256), 256)
        result = lax.dot_general(
            wyx[...], wz[at, :], (((1,), (1,)), ((), ())), preferred_element_type=jnp.float32
        )
        acc[0, :, at] = result[:width_y]
        acc[1, :, at] = result[width_y:]
        return carry

    lax.fori_loop(0, width_z // 256, spread_source, 0)
    faces(2)

    p_copy.wait_recv()
    r_copy.wait_recv()
    inner = (1 - bi).astype(jnp.float32)
    for plane in range(planes):
        p_lower, r_lower = p_edge[plane, 7:8, :], r_edge[plane, 7:8, :]
        p_upper, r_upper = p_edge[plane, 0:1, :], r_edge[plane, 0:1, :]
        pv[plane, 7:8, :] = p_lower
        rv[plane, 7:8, :] = r_lower + inner * FAR
        pv[plane, HALO + width_y : HALO + width_y + 1, :] = p_upper
        rv[plane, HALO + width_y : HALO + width_y + 1, :] = r_upper + (1.0 - inner) * FAR

    def stencil(step, carry):
        y = pl.multiple_of(step * 8, 8)
        p = [pv[plane, pl.ds(HALO + y, 8), :] for plane in range(planes)]
        r = [rv[plane, pl.ds(HALO + y, 8), :] for plane in range(planes)]
        last = lax.broadcasted_iota(jnp.int32, (8, width_z), 1) == width_z - 1
        between = (p[1] - p[0]) * inverse(r[0] + r[1])
        for plane in range(planes):
            pc, rc = p[plane], r[plane]
            total = acc[plane, pl.ds(y, 8), :]
            total = total + between if plane == 0 else total - between
            for shift in (1, -1):
                pn = pv.at[plane, pl.ds(y, 24), :][HALO + shift : HALO + shift + 8, :]
                rn = rv.at[plane, pl.ds(y, 24), :][HALO + shift : HALO + shift + 8, :]
                total = total + (pn - pc) * inverse(rn + rc)
            pn = pltpu.roll(pc, width_z - 1, 1)
            rn = pltpu.roll(rc, width_z - 1, 1)
            flux = jnp.where(last, jnp.float32(0.0), (pn - pc) * inverse(rn + rc))
            total = total + flux - pltpu.roll(flux, 1, 1)
            acc[plane, pl.ds(y, 8), :] = total
        return carry

    lax.fori_loop(0, width_y // 8, stencil, 0)
    faces(3)

    tot_copy.wait_recv()
    near_copy.wait_recv()
    fp_copy.wait_recv()
    totals = tot_own[...] + tot_other[...]
    for c in range(4):
        basis = row_basis[:, 512 * c : 512 * (c + 1)].astype(jnp.float32)
        store_rows(
            far16, 4 * c, jnp.sum(basis * totals[:, c : c + 1], axis=0, keepdims=True)
        )
    own, others = near_own[...], near_other[...]
    first = bi == 0
    near16 = jnp.concatenate(
        [jnp.where(first, own, others), jnp.where(first, others, own)], axis=0
    )
    traction = near16 + far16[...]
    effective = stress[...] - (fp_own[...] + fp_other[...])
    rate = slip[...]
    state_rate = jnp.exp(-log_state[...]) - rate
    accel_out[...] = (traction - effective * friction_b[...] * state_rate) / (
        effective * friction_a[...] / rate + 0.5
    )
    state_out[...] = state_rate

    stores = []
    for part in range(PARTS):
        low = pl.ds(part * rows, rows)
        high = pl.ds(half + part * rows, rows)
        for which, plane, at, flux in (
            (0, 0, low, fsnd.at[0, part]),
            (1, 1, high, fsnd.at[1, part]),
        ):
            value = flux[...].astype(jnp.float32)
            acc[plane, at, :] = acc[plane, at, :] + value
            copy = pltpu.make_async_copy(
                acc.at[plane, at], rate_hbm.at[plane, at], out_sem.at[which, part]
            )
            copy.start()
            stores.append(copy)
    for part in range(PARTS):
        low = pl.ds(part * rows, rows)
        high = pl.ds(half + part * rows, rows)
        for which, plane, at, way in ((2, 1, low, 0), (3, 0, high, 1)):
            fl_copies[way, part].wait_recv()
            value = frcv[way, part].astype(jnp.float32)
            acc[plane, at, :] = acc[plane, at, :] - value
            copy = pltpu.make_async_copy(
                acc.at[plane, at], rate_hbm.at[plane, at], out_sem.at[which, part]
            )
            copy.start()
            stores.append(copy)
    for copy in stores:
        copy.wait()
    sent = x_copies + z_copies + y_copies + pr_copies + list(fl_copies.values())
    for copy in sent + [slip_up, slip_down, p_copy, r_copy, fp_copy, near_copy, tot_copy]:
        copy.wait_send()


def shards(
    slip_rate,
    log_state,
    friction_a,
    friction_b,
    normal_stress,
    leak_rate,
    corner,
    fraction,
    near_blocks,
    row_basis,
    col_basis,
    far_row,
    far_col,
    far_rank,
    far_coupling,
    pressure,
    region,
    perm_table,
):
    sizes = tuple(lax.axis_size(name) for name in SLAB)
    ny, nz, nx = sizes
    planes, width_y, width_z = pressure.shape
    cells = slip_rate.shape[0]
    clusters = cells // 512
    slots = far_row.shape[0]
    rank = col_basis.shape[0]
    rows = width_y // 2 // PARTS
    f32, bf16 = jnp.float32, jnp.bfloat16
    table = jnp.broadcast_to(
        jnp.pad(0.5 / perm_table, (0, 128 - perm_table.shape[0])), (8, 128)
    )
    vmem = pl.BlockSpec(memory_space=pltpu.VMEM)
    hbm = pl.BlockSpec(memory_space=pl.ANY)
    dma = pltpu.SemaphoreType.DMA

    def cut(x):
        return x.reshape(-1, 128)

    rate, accel, state = pl.pallas_call(
        functools.partial(kernel, sizes),
        out_shape=(
            jax.ShapeDtypeStruct(pressure.shape, f32),
            jax.ShapeDtypeStruct((cells // 128, 128), f32),
            jax.ShapeDtypeStruct((cells // 128, 128), f32),
        ),
        in_specs=[vmem] * 14 + [hbm] * 4,
        out_specs=(hbm, vmem, vmem),
        scratch_shapes=[
            pltpu.VMEM((planes, width_y + 2 * HALO, width_z), f32),
            pltpu.VMEM((planes, width_y + 2 * HALO, width_z), f32),
            pltpu.VMEM((planes, width_y, width_z), jnp.int32),
            pltpu.VMEM((planes, width_y, width_z), f32),
            pltpu.VMEM((2, PARTS, 2, rows, width_z), bf16),
            pltpu.VMEM((2, PARTS, 2, rows, width_z), bf16),
            pltpu.VMEM((2, PARTS, rows, width_z), bf16),
            pltpu.VMEM((2, PARTS, rows, width_z), bf16),
            pltpu.VMEM((planes, 8, width_z), f32),
            pltpu.VMEM((planes, 8, width_z), f32),
            pltpu.VMEM((width_z, cells), bf16),
            pltpu.VMEM((planes * width_y, cells), bf16),
            pltpu.VMEM((planes * width_y, width_z), bf16),
            pltpu.VMEM(near_blocks.shape, bf16),
            pltpu.VMEM(far_coupling.shape, bf16),
            pltpu.VMEM((ny * nz * nx * clusters, slots), bf16),
            pltpu.VMEM((nx, 8, 128), f32),
            pltpu.VMEM((ny, nz, nx * clusters, 128), bf16),
            pltpu.VMEM((2, 8, 128), f32),
            pltpu.VMEM((8, 512), f32),
            pltpu.VMEM((1, cells), f32),
            pltpu.VMEM((1, cells), f32),
            pltpu.VMEM((cells // 128, 128), f32),
            pltpu.VMEM((cells // 128, 128), f32),
            pltpu.VMEM((8, 128), f32),
            pltpu.VMEM((8, 128), f32),
            pltpu.VMEM((rank, 128), f32),
            pltpu.VMEM((rank, 128), f32),
            pltpu.VMEM((rank, slots), f32),
            pltpu.VMEM((cells // 128, 128), f32),
            dma((10,)),
            dma((nx - 1,)),
            dma((nx - 1,)),
            dma((nz - 1,)),
            dma((nz - 1,)),
            dma((ny - 1,)),
            dma((ny - 1,)),
            dma((2, PARTS)),
            dma((2, PARTS)),
            dma((2, PARTS)),
            dma((2, PARTS)),
            dma((7,)),
            dma((7,)),
            dma((4, PARTS)),
        ],
        compiler_params=pltpu.CompilerParams(
            collective_id=0, has_side_effects=True, vmem_limit_bytes=48 * 1024 * 1024
        ),
        name="fault_step",
    )(
        cut(slip_rate),
        cut(log_state),
        cut(friction_a),
        cut(friction_b),
        cut(normal_stress),
        cut(leak_rate),
        corner,
        fraction,
        row_basis,
        col_basis,
        cut(far_row),
        cut(far_col),
        cut(far_rank),
        table,
        near_blocks,
        far_coupling,
        pressure,
        region,
    )
    return accel.reshape(cells), state.reshape(cells), rate


def solution(mesh):
    torus = Mesh(
        mesh.devices.reshape(4, 8, 4, mesh.shape["blk"]), ("slab_0", "slab_1", "slab_2", "blk")
    )
    placed = (
        P(SLAB),
        P(SLAB),
        P(SLAB),
        P(SLAB),
        P(SLAB),
        P(SLAB),
        P(None, SLAB),
        P(None, SLAB),
        P(SLAB_BLK, None, None, None),
        P(None, SLAB),
        P(None, SLAB),
        P(SLAB_BLK),
        P(SLAB_BLK),
        P(SLAB_BLK),
        P(None, None, SLAB_BLK),
        P(SLAB, "blk", None),
        P(SLAB, "blk", None),
        P(),
    )
    return jax.shard_map(
        shards,
        mesh=torus,
        in_specs=placed,
        out_specs=(P(SLAB), P(SLAB), P(SLAB, "blk", None)),
        check_vma=False,
    )
```

profile of v0, /device:TPU:1, one launch (start us, length us, event | category | flops | bytes accessed | tf_op | source)
XLA Modules:
  0.0 64.4 jit_solution(13513304425450200713)
XLA Ops:
  0.6 0.7 %broadcast_divide_fusion = f32[16]{0:T(128)S(1)} fusion(f32[16]{0:T(128)} %param.35), kind=kLoop, calls=%fused_computation | loop fusion | flops 16 | bytes 128 | tf_op jit(solution)/shard_map/div | solution.py:521
  1.3 0.0 copy-start
  1.3 1.6 %copy-done = f32[2,256,1024]{2,1,0:T(8,128)S(1)} copy-done((f32[2,256,1024]{2,1,0:T(8,128)S(1)}, f32[2,256,1024]{2,1,0:T(8,128)}, u32[]{:S(2)}) %copy-start) | copy-done | bytes 2097176
  2.9 0.0 copy-start.1
  2.9 1.3 %copy-done.1 = bf16[24,24,1024]{2,1,0:T(8,128)(2,1)S(1)} copy-done((bf16[24,24,1024]{2,1,0:T(8,128)(2,1)S(1)}, bf16[24,24,1024]{2,1,0:T(8,128)(2,1)}, u32[]{:S(2)}) %copy-start.1) | copy-done | bytes 1179672
  4.2 0.0 copy-start.2
  4.2 0.9 %copy-done.2 = bf16[24,2048]{1,0:T(8,128)(2,1)S(1)} copy-done((bf16[24,2048]{1,0:T(8,128)(2,1)S(1)}, bf16[24,2048]{1,0:T(8,128)(2,1)}, u32[]{:S(2)}) %copy-start.2) | copy-done | bytes 98328
  5.1 0.0 copy-start.3
  5.1 0.9 %copy-done.3 = bf16[24,2048]{1,0:T(8,128)(2,1)S(1)} copy-done((bf16[24,2048]{1,0:T(8,128)(2,1)S(1)}, bf16[24,2048]{1,0:T(8,128)(2,1)}, u32[]{:S(2)}) %copy-start.3) | copy-done | bytes 98328
  6.0 0.8 %copy-done.4 = s32[3,2048]{1,0:T(4,128)S(1)} copy-done((s32[3,2048]{1,0:T(4,128)S(1)}, s32[3,2048]{1,0:T(4,128)}, u32[]{:S(2)}) %copy-start.4) | copy-done | bytes 24600
  6.7 0.8 %copy-done.5 = f32[3,2048]{1,0:T(4,128)S(1)} copy-done((f32[3,2048]{1,0:T(4,128)S(1)}, f32[3,2048]{1,0:T(4,128)}, u32[]{:S(2)}) %copy-start.5) | copy-done | bytes 24600
  7.5 0.7 %copy-done.6 = f32[2048]{0:T(1024)S(1)} copy-done((f32[2048]{0:T(1024)S(1)}, f32[2048]{0:T(1024)}, u32[]{:S(2)}) %copy-start.6) | copy-done | bytes 8216
  8.2 0.7 %copy-done.7 = f32[2048]{0:T(1024)S(1)} copy-done((f32[2048]{0:T(1024)S(1)}, f32[2048]{0:T(1024)}, u32[]{:S(2)}) %copy-start.7) | copy-done | bytes 8216
  8.9 0.7 %copy-done.8 = f32[2048]{0:T(1024)S(1)} copy-done((f32[2048]{0:T(1024)S(1)}, f32[2048]{0:T(1024)}, u32[]{:S(2)}) %copy-start.8) | copy-done | bytes 8216
  9.6 0.7 %copy-done.9 = f32[2048]{0:T(1024)S(1)} copy-done((f32[2048]{0:T(1024)S(1)}, f32[2048]{0:T(1024)}, u32[]{:S(2)}) %copy-start.9) | copy-done | bytes 8216
  10.3 0.7 %copy-done.10 = f32[2048]{0:T(1024)S(1)} copy-done((f32[2048]{0:T(1024)S(1)}, f32[2048]{0:T(1024)}, u32[]{:S(2)}) %copy-start.10) | copy-done | bytes 8216
  11.0 0.7 %copy-done.11 = f32[2048]{0:T(1024)S(1)} copy-done((f32[2048]{0:T(1024)S(1)}, f32[2048]{0:T(1024)}, u32[]{:S(2)}) %copy-start.11) | copy-done | bytes 8216
  11.7 0.7 %copy-done.12 = s32[1024]{0:T(1024)S(1)} copy-done((s32[1024]{0:T(1024)S(1)}, s32[1024]{0:T(1024)}, u32[]{:S(2)}) %copy-start.12) | copy-done | bytes 4120
  12.3 0.7 %copy-done.13 = s32[1024]{0:T(1024)S(1)} copy-done((s32[1024]{0:T(1024)S(1)}, s32[1024]{0:T(1024)}, u32[]{:S(2)}) %copy-start.13) | copy-done | bytes 4120
  13.0 0.7 %copy-done.14 = s32[1024]{0:T(1024)S(1)} copy-done((s32[1024]{0:T(1024)S(1)}, s32[1024]{0:T(1024)}, u32[]{:S(2)}) %copy-start.14) | copy-done | bytes 4120
  13.7 48.2 %fault_step.1 = (f32[2,256,1024]{2,1,0:T(8,128)S(1)}, f32[16,128]{1,0:T(8,128)S(1)}, f32[16,128]{1,0:T(8,128)S(1)}) custom-call(f32[16,128]{1,0:T(8,128)S(1)} %bitcast.13, f32[16,128]{1,0:T(8,128)S(1)} %bitcast.14, f32[16,128]{1,0:T(8,128)S(1)} %bitcast.15, f32[16,128]{1,0:T(8,128)S(1)} %bitcast.16, f32[16,128]{1,0:T(8,128)S(1)} %bitcast.17, ...), custom_call_target="tpu_custom_call" | custom-call | tf_op jit(solution)/shard_map/fault_step/pallas_call | solution.py:530
  61.9 0.6 copy.24
  62.5 0.6 copy.25
  63.1 1.3 %copy.26 = f32[2,256,1024]{2,1,0:T(8,128)} copy(f32[2,256,1024]{2,1,0:T(8,128)S(1)} %get-tuple-element.14) | data formatting | bytes 4194304
  (13 shorter events, 0.0 us)
Async XLA Ops:
  1.3 1.6 %copy-start = (f32[2,256,1024]{2,1,0:T(8,128)S(1)}, f32[2,256,1024]{2,1,0:T(8,128)}, u32[]{:S(2)}) copy-start(f32[2,256,1024]{2,1,0:T(8,128)} %p_hbm.1) | copy-start | bytes 6291460
  2.9 1.3 %copy-start.1 = (bf16[24,24,1024]{2,1,0:T(8,128)(2,1)S(1)}, bf16[24,24,1024]{2,1,0:T(8,128)(2,1)}, u32[]{:S(2)}) copy-start(bf16[24,24,1024]{2,1,0:T(8,128)(2,1)} %coupling_hbm.1) | copy-start | bytes 3538948
  4.2 0.9 %copy-start.2 = (bf16[24,2048]{1,0:T(8,128)(2,1)S(1)}, bf16[24,2048]{1,0:T(8,128)(2,1)}, u32[]{:S(2)}) copy-start(bf16[24,2048]{1,0:T(8,128)(2,1)} %row_basis.1) | copy-start | bytes 294916
  5.1 0.9 %copy-start.3 = (bf16[24,2048]{1,0:T(8,128)(2,1)S(1)}, bf16[24,2048]{1,0:T(8,128)(2,1)}, u32[]{:S(2)}) copy-start(bf16[24,2048]{1,0:T(8,128)(2,1)} %col_basis.1) | copy-start | bytes 294916
  6.0 0.8 %copy-start.4 = (s32[3,2048]{1,0:T(4,128)S(1)}, s32[3,2048]{1,0:T(4,128)}, u32[]{:S(2)}) copy-start(s32[3,2048]{1,0:T(4,128)} %corner.1) | copy-start | bytes 73732
  6.7 0.8 %copy-start.5 = (f32[3,2048]{1,0:T(4,128)S(1)}, f32[3,2048]{1,0:T(4,128)}, u32[]{:S(2)}) copy-start(f32[3,2048]{1,0:T(4,128)} %fraction.1) | copy-start | bytes 73732
  7.5 0.7 %copy-start.6 = (f32[2048]{0:T(1024)S(1)}, f32[2048]{0:T(1024)}, u32[]{:S(2)}) copy-start(f32[2048]{0:T(1024)} %param.18) | copy-start | bytes 24580
  8.2 0.7 %copy-start.7 = (f32[2048]{0:T(1024)S(1)}, f32[2048]{0:T(1024)}, u32[]{:S(2)}) copy-start(f32[2048]{0:T(1024)} %param.19) | copy-start | bytes 24580
  8.9 0.7 %copy-start.8 = (f32[2048]{0:T(1024)S(1)}, f32[2048]{0:T(1024)}, u32[]{:S(2)}) copy-start(f32[2048]{0:T(1024)} %param.20) | copy-start | bytes 24580
  9.6 0.7 %copy-start.9 = (f32[2048]{0:T(1024)S(1)}, f32[2048]{0:T(1024)}, u32[]{:S(2)}) copy-start(f32[2048]{0:T(1024)} %param.21) | copy-start | bytes 24580
  10.3 0.7 %copy-start.10 = (f32[2048]{0:T(1024)S(1)}, f32[2048]{0:T(1024)}, u32[]{:S(2)}) copy-start(f32[2048]{0:T(1024)} %param.22) | copy-start | bytes 24580
  11.0 0.7 %copy-start.11 = (f32[2048]{0:T(1024)S(1)}, f32[2048]{0:T(1024)}, u32[]{:S(2)}) copy-start(f32[2048]{0:T(1024)} %param.23) | copy-start | bytes 24580
  11.7 0.7 %copy-start.12 = (s32[1024]{0:T(1024)S(1)}, s32[1024]{0:T(1024)}, u32[]{:S(2)}) copy-start(s32[1024]{0:T(1024)} %param.29) | copy-start | bytes 12292
  12.3 0.7 %copy-start.13 = (s32[1024]{0:T(1024)S(1)}, s32[1024]{0:T(1024)}, u32[]{:S(2)}) copy-start(s32[1024]{0:T(1024)} %param.30) | copy-start | bytes 12292
  13.0 0.7 %copy-start.14 = (s32[1024]{0:T(1024)S(1)}, s32[1024]{0:T(1024)}, u32[]{:S(2)}) copy-start(s32[1024]{0:T(1024)} %param.31) | copy-start | bytes 12292
where the time goes:
time: 65.1 us; the launch traced here: 64.4 us
  Pallas kernels  48.2 us (74%)
  local copies, waits for them, and re-layouts  14.9 us (23%)
  other arithmetic  0.66 us (1%)
  between operations  0.66 us (1%)
    pallas_call x1, Pallas kernels, shards(): pl.pallas_call(functools.partial(kernel, sizes), out_shape=(jax.ShapeDtyp...  48.2 us
    unnamed x33, local copies, waits for them, and re-layouts  14.9 us

commit v1 on v0

--- a/solution.py
+++ b/solution.py
@@ -33,6 +33,27 @@
 
 def kernel(
     sizes,
+    slip_hbm,
+    log_state_hbm,
+    friction_a_hbm,
+    friction_b_hbm,
+    stress_hbm,
+    leak_hbm,
+    corner_hbm,
+    fraction_hbm,
+    row_basis_hbm,
+    col_basis_hbm,
+    far_row_hbm,
+    far_col_hbm,
+    far_rank_hbm,
+    table_hbm,
+    near_hbm,
+    coupling_hbm,
+    p_hbm,
+    region_hbm,
+    rate_hbm,
+    accel_out,
+    state_out,
     slip,
     log_state,
     friction_a,
@@ -47,13 +68,6 @@
     far_col,
     far_rank,
     table,
-    near_hbm,
-    coupling_hbm,
-    p_hbm,
-    region_hbm,
-    rate_hbm,
-    accel_out,
-    state_out,
     pv,
     rv,
     region,
@@ -152,10 +166,38 @@
 
     first_up, first_down = quarter(1, 0, 0), quarter(0, 1, 2)
     later = quarter(0, 0, 4) + quarter(1, 1, 6)
+    small = [
+        pltpu.make_async_copy(src, dst, load_sem.at[10 + i])
+        for i, (src, dst) in enumerate(
+            (
+                (slip_hbm, slip),
+                (col_basis_hbm, col_basis),
+                (table_hbm, table),
+                (leak_hbm, leak),
+                (corner_hbm, corner),
+                (fraction_hbm, fraction),
+                (far_col_hbm, far_col),
+                (far_rank_hbm, far_rank),
+                (far_row_hbm, far_row),
+                (row_basis_hbm, row_basis),
+                (stress_hbm, stress),
+                (log_state_hbm, log_state),
+                (friction_a_hbm, friction_a),
+                (friction_b_hbm, friction_b),
+            )
+        )
+    ]
     load_near = pltpu.make_async_copy(near_hbm, near, load_sem.at[8])
     load_coupling = pltpu.make_async_copy(coupling_hbm, coupling, load_sem.at[9])
-    for copy in first_up + first_down + later + (load_near, load_coupling):
+    ahead = small[:4]
+    behind = small[4:6]
+    last = small[6:]
+    for copy in ahead[:3] + list(first_up + first_down) + ahead[3:] + behind + list(later):
         copy.start()
+    for copy in [load_near, load_coupling] + last:
+        copy.start()
+    for copy in ahead:
+        copy.wait()
 
     for c in range(4):
         window[1 + c : 2 + c, :] = lanes_row(slip, 4 * c, 4)
@@ -187,9 +229,11 @@
     slip_up.start()
     slip_down.start()
 
+    halves = jnp.concatenate([0.5 / table[...], jnp.zeros((1, 128 - table.shape[1]), jnp.float32)], axis=1)
+
     def look_up(plane, start, count):
         chosen = region[plane, pl.ds(start, count), :]
-        entries = jnp.broadcast_to(table[0:1, :], (count, 128))
+        entries = jnp.broadcast_to(halves, (count, 128))
         r = jnp.concatenate(
             [
                 jnp.take_along_axis(
@@ -229,7 +273,7 @@
             copy.start()
             pr_copies.append(copy)
 
-    for copy in later:
+    for copy in later + tuple(behind):
         copy.wait()
 
     def rest(step, carry):
@@ -353,6 +397,8 @@
     near_copy = remote(near_own, near_other, one_send.at[5], one_recv.at[5], other)
     near_copy.start()
 
+    for copy in last:
+        copy.wait()
     column = lanes_row(far_col, 0, 8)
     pick[...] = jnp.where(
         lax.broadcasted_iota(jnp.int32, pick.shape, 0) == column, 1.0, 0.0
@@ -517,9 +563,6 @@
     rank = col_basis.shape[0]
     rows = width_y // 2 // PARTS
     f32, bf16 = jnp.float32, jnp.bfloat16
-    table = jnp.broadcast_to(
-        jnp.pad(0.5 / perm_table, (0, 128 - perm_table.shape[0])), (8, 128)
-    )
     vmem = pl.BlockSpec(memory_space=pltpu.VMEM)
     hbm = pl.BlockSpec(memory_space=pl.ANY)
     dma = pltpu.SemaphoreType.DMA
@@ -534,9 +577,16 @@
             jax.ShapeDtypeStruct((cells // 128, 128), f32),
             jax.ShapeDtypeStruct((cells // 128, 128), f32),
         ),
-        in_specs=[vmem] * 14 + [hbm] * 4,
+        in_specs=[hbm] * 18,
         out_specs=(hbm, vmem, vmem),
         scratch_shapes=[
+            *[pltpu.VMEM((cells // 128, 128), f32)] * 6,
+            pltpu.VMEM(corner.shape, jnp.int32),
+            pltpu.VMEM(fraction.shape, f32),
+            pltpu.VMEM(row_basis.shape, bf16),
+            pltpu.VMEM(col_basis.shape, bf16),
+            *[pltpu.VMEM((slots // 128, 128), jnp.int32)] * 3,
+            pltpu.VMEM((1, perm_table.shape[0]), f32),
             pltpu.VMEM((planes, width_y + 2 * HALO, width_z), f32),
             pltpu.VMEM((planes, width_y + 2 * HALO, width_z), f32),
             pltpu.VMEM((planes, width_y, width_z), jnp.int32),
@@ -567,7 +617,7 @@
             pltpu.VMEM((rank, 128), f32),
             pltpu.VMEM((rank, slots), f32),
             pltpu.VMEM((cells // 128, 128), f32),
-            dma((10,)),
+            dma((24,)),
             dma((nx - 1,)),
             dma((nx - 1,)),
             dma((nz - 1,)),
@@ -583,7 +633,7 @@
             dma((4, PARTS)),
         ],
         compiler_params=pltpu.CompilerParams(
-            collective_id=0, has_side_effects=True, vmem_limit_bytes=48 * 1024 * 1024
+            collective_id=0, has_side_effects=True, vmem_limit_bytes=60 * 1024 * 1024
         ),
         name="fault_step",
     )(
@@ -600,7 +650,7 @@
         cut(far_row),
         cut(far_col),
         cut(far_rank),
-        table,
+        perm_table.reshape(1, -1),
         near_blocks,
         far_coupling,
         pressure,

time: 65.1 us -> 56.3 us (0.86)
  local copies, waits for them, and re-layouts: 14.9 us -> 5.75 us
  Pallas kernels: 48.2 us -> 49.6 us
  other arithmetic: 0.66 us -> 0 us
    unnamed x33 -> x3, local copies, waits for them, and re-layouts: 14.9 us -> 5.75 us
    pallas_call x1, Pallas kernels: 48.2 us -> 49.6 us  [shards(): pl.pallas_call(functools.partial(kernel, sizes), out_shape=(jax.ShapeDtyp...]
    div x1 -> x0, other arithmetic: 0.66 us -> none  [shards(): 0.5 / perm_table]
where the time goes in v1:
time: 56.3 us; the launch traced here: 56 us
  Pallas kernels  49.6 us (88%)
  local copies, waits for them, and re-layouts  5.75 us (10%)
  between operations  0.65 us (1%)
    pallas_call x1, Pallas kernels, shards(): pl.pallas_call(functools.partial(kernel, sizes), out_shape=(jax.ShapeDtyp...  49.6 us
    unnamed x3, local copies, waits for them, and re-layouts  5.75 us

profile of v1, /device:TPU:1, one launch (start us, length us, event | category | flops | bytes accessed | tf_op | source)
XLA Modules:
  0.0 56.0 jit_solution(13948997485695681723)
XLA Ops:
  0.6 49.6 %fault_step.1 = (f32[2,256,1024]{2,1,0:T(8,128)}, f32[16,128]{1,0:T(8,128)}, f32[16,128]{1,0:T(8,128)}) custom-call(f32[16,128]{1,0:T(8,128)} %bitcast.12, f32[16,128]{1,0:T(8,128)} %bitcast.13, f32[16,128]{1,0:T(8,128)} %bitcast.14, f32[16,128]{1,0:T(8,128)} %bitcast.15, f32[16,128]{1,0:T(8,128)} %bitcast.16, f32[16,128]{1,0:T(8,128)} %bitcast.17, ...), custom_call_target="tpu_custom_call" | custom-call | tf_op jit(solution)/shard_map/fault_step/pallas_call | solution.py:573
  50.2 1.3 %copy.24 = f32[2048]{0:T(1024)} copy(f32[2048]{0:T(1024)} %bitcast.19) | data formatting | bytes 16384
  51.5 1.3 %copy.25 = f32[2048]{0:T(1024)} copy(f32[2048]{0:T(1024)} %bitcast.18) | data formatting | bytes 16384
  52.8 3.2 %copy.26 = f32[2,256,1024]{2,1,0:T(8,128)} copy(f32[2,256,1024]{2,1,0:T(8,128)} %get-tuple-element.14) | data formatting | bytes 4194304

commit v2 on v1

--- a/solution.py
+++ b/solution.py
@@ -13,7 +13,8 @@
 MESH = pl.DeviceIdType.MESH
 
 PARTS = 4
-F_TILE = 256
+F_TILE = 512
+Z_TILE = 256
 HALO = 8
 FAR = 1e30
 
@@ -72,6 +73,7 @@
     rv,
     region,
     acc,
+    source,
     snd,
     rcv,
     fsnd,
@@ -294,27 +296,19 @@
     p_copy.start()
     r_copy.start()
 
-    for copy in x_copies:
-        copy.wait_recv()
-    mine = jnp.concatenate([gather_x[i, 0:4, :] for i in range(nx)], axis=0)
-    gather[yi, zi] = mine.astype(jnp.bfloat16)
-    z_copies = [
-        remote(gather.at[yi, zi], gather.at[yi, zi], z_send.at[d], z_recv.at[d], peer)
-        for d, peer in enumerate(z_peers)
-    ]
-    for copy in z_copies:
-        copy.start()
-
     y_start = bi * width_y
 
     def sample(step, carry):
         at = pl.ds(pl.multiple_of(step * F_TILE, F_TILE), F_TILE)
         z = corner[2:3, at]
         fz = fraction[2:3, at]
-        iota = lax.broadcasted_iota(jnp.int32, (width_z, F_TILE), 0)
+        iota = lax.broadcasted_iota(jnp.int16, (width_z, F_TILE), 0)
+        z = jnp.broadcast_to(z, (16, F_TILE)).astype(jnp.int16)[0:1]
         weight = jnp.where(
-            iota == z, 1.0 - fz, jnp.where(iota == z + 1, fz, jnp.float32(0.0))
-        ).astype(jnp.bfloat16)
+            iota == z,
+            (1.0 - fz).astype(jnp.bfloat16),
+            jnp.where(iota == z + 1, fz.astype(jnp.bfloat16), jnp.bfloat16(0.0)),
+        )
         wz[:, at] = weight
         along_z = jnp.dot(p_low[...], weight, preferred_element_type=jnp.float32)
         y = corner[1:2, at] - y_start
@@ -331,15 +325,17 @@
         return carry
 
     steps = cells // F_TILE
-    lax.fori_loop(0, steps // 2, sample, 0)
-
+    lax.fori_loop(0, 1, sample, 0)
+
+    for copy in x_copies:
+        copy.wait_recv()
+    mine = jnp.concatenate([gather_x[i, 0:4, :] for i in range(nx)], axis=0)
+    gather[yi, zi] = mine.astype(jnp.bfloat16)
+    z_copies = [
+        remote(gather.at[yi, zi], gather.at[yi, zi], z_send.at[d], z_recv.at[d], peer)
+        for d, peer in enumerate(z_peers)
+    ]
     for copy in z_copies:
-        copy.wait_recv()
-    y_copies = [
-        remote(gather.at[yi], gather.at[yi], y_send.at[d], y_recv.at[d], peer)
-        for d, peer in enumerate(y_peers)
-    ]
-    for copy in y_copies:
         copy.start()
 
     has_below = jnp.where(slab > 0, 1.0, 0.0).astype(jnp.float32)
@@ -368,13 +364,22 @@
             copy.start()
             fl_copies[way, part] = copy
 
+    lax.fori_loop(1, 3, sample, 0)
     faces(0)
-    lax.fori_loop(steps // 2, steps, sample, 0)
+    lax.fori_loop(3, steps, sample, 0)
     for c in range(16):
         fp_own[c : c + 1, :] = fp_row[:, 128 * c : 128 * (c + 1)]
     fp_copy = remote(fp_own, fp_other, one_send.at[4], one_recv.at[4], other)
     fp_copy.start()
-    faces(1)
+
+    for copy in z_copies:
+        copy.wait_recv()
+    y_copies = [
+        remote(gather.at[yi], gather.at[yi], y_send.at[d], y_recv.at[d], peer)
+        for d, peer in enumerate(y_peers)
+    ]
+    for copy in y_copies:
+        copy.start()
 
     slip_up.wait_recv()
     slip_down.wait_recv()
@@ -396,6 +401,53 @@
         store_rows(near_own, 4 * i, total[0:1, :])
     near_copy = remote(near_own, near_other, one_send.at[5], one_recv.at[5], other)
     near_copy.start()
+    faces(1)
+
+    p_copy.wait_recv()
+    r_copy.wait_recv()
+    inner = (1 - bi).astype(jnp.float32)
+    for plane in range(planes):
+        p_lower, r_lower = p_edge[plane, 7:8, :], r_edge[plane, 7:8, :]
+        p_upper, r_upper = p_edge[plane, 0:1, :], r_edge[plane, 0:1, :]
+        pv[plane, 7:8, :] = p_lower
+        rv[plane, 7:8, :] = r_lower + inner * FAR
+        pv[plane, HALO + width_y : HALO + width_y + 1, :] = p_upper
+        rv[plane, HALO + width_y : HALO + width_y + 1, :] = r_upper + (1.0 - inner) * FAR
+
+    def stencil(y):
+        p = [pv[plane, pl.ds(HALO + y, 8), :] for plane in range(planes)]
+        r = [rv[plane, pl.ds(HALO + y, 8), :] for plane in range(planes)]
+        last = lax.broadcasted_iota(jnp.int32, (8, width_z), 1) == width_z - 1
+        between = (p[1] - p[0]) * inverse(r[0] + r[1])
+        for plane in range(planes):
+            pc, rc = p[plane], r[plane]
+            total = between if plane == 0 else -between
+            for shift in (1, -1):
+                pn = pv.at[plane, pl.ds(y, 24), :][HALO + shift : HALO + shift + 8, :]
+                rn = rv.at[plane, pl.ds(y, 24), :][HALO + shift : HALO + shift + 8, :]
+                total = total + (pn - pc) * inverse(rn + rc)
+            pn = pltpu.roll(pc, width_z - 1, 1)
+            rn = pltpu.roll(rc, width_z - 1, 1)
+            flux = jnp.where(last, jnp.float32(0.0), (pn - pc) * inverse(rn + rc))
+            total = total + flux - pltpu.roll(flux, 1, 1)
+            acc[plane, pl.ds(y, 8), :] = total
+
+    def spread_source(step, carry):
+        at = pl.ds(pl.multiple_of(step * Z_TILE, Z_TILE), Z_TILE)
+        result = lax.dot_general(
+            wyx[...], wz[at, :], (((1,), (1,)), ((), ())), preferred_element_type=jnp.float32
+        )
+        source[0, :, at] = result[:width_y]
+        source[1, :, at] = result[width_y:]
+        count = width_y // 8 // (width_z // Z_TILE)
+        for k in range(count):
+            stencil(pl.multiple_of((step * count + k) * 8, 8))
+        return carry
+
+    spreads = width_z // Z_TILE
+    lax.fori_loop(0, spreads // 2, spread_source, 0)
+    faces(2)
+    faces(3)
 
     for copy in last:
         copy.wait()
@@ -430,52 +482,7 @@
     tot_copy = remote(tot_own, tot_other, one_send.at[6], one_recv.at[6], other)
     tot_copy.start()
 
-    def spread_source(step, carry):
-        at = pl.ds(pl.multiple_of(step * 256, 256), 256)
-        result = lax.dot_general(
-            wyx[...], wz[at, :], (((1,), (1,)), ((), ())), preferred_element_type=jnp.float32
-        )
-        acc[0, :, at] = result[:width_y]
-        acc[1, :, at] = result[width_y:]
-        return carry
-
-    lax.fori_loop(0, width_z // 256, spread_source, 0)
-    faces(2)
-
-    p_copy.wait_recv()
-    r_copy.wait_recv()
-    inner = (1 - bi).astype(jnp.float32)
-    for plane in range(planes):
-        p_lower, r_lower = p_edge[plane, 7:8, :], r_edge[plane, 7:8, :]
-        p_upper, r_upper = p_edge[plane, 0:1, :], r_edge[plane, 0:1, :]
-        pv[plane, 7:8, :] = p_lower
-        rv[plane, 7:8, :] = r_lower + inner * FAR
-        pv[plane, HALO + width_y : HALO + width_y + 1, :] = p_upper
-        rv[plane, HALO + width_y : HALO + width_y + 1, :] = r_upper + (1.0 - inner) * FAR
-
-    def stencil(step, carry):
-        y = pl.multiple_of(step * 8, 8)
-        p = [pv[plane, pl.ds(HALO + y, 8), :] for plane in range(planes)]
-        r = [rv[plane, pl.ds(HALO + y, 8), :] for plane in range(planes)]
-        last = lax.broadcasted_iota(jnp.int32, (8, width_z), 1) == width_z - 1
-        between = (p[1] - p[0]) * inverse(r[0] + r[1])
-        for plane in range(planes):
-            pc, rc = p[plane], r[plane]
-            total = acc[plane, pl.ds(y, 8), :]
-            total = total + between if plane == 0 else total - between
-            for shift in (1, -1):
-                pn = pv.at[plane, pl.ds(y, 24), :][HALO + shift : HALO + shift + 8, :]
-                rn = rv.at[plane, pl.ds(y, 24), :][HALO + shift : HALO + shift + 8, :]
-                total = total + (pn - pc) * inverse(rn + rc)
-            pn = pltpu.roll(pc, width_z - 1, 1)
-            rn = pltpu.roll(rc, width_z - 1, 1)
-            flux = jnp.where(last, jnp.float32(0.0), (pn - pc) * inverse(rn + rc))
-            total = total + flux - pltpu.roll(flux, 1, 1)
-            acc[plane, pl.ds(y, 8), :] = total
-        return carry
-
-    lax.fori_loop(0, width_y // 8, stencil, 0)
-    faces(3)
+    lax.fori_loop(spreads // 2, spreads, spread_source, 0)
 
     tot_copy.wait_recv()
     near_copy.wait_recv()
@@ -509,7 +516,7 @@
             (1, 1, high, fsnd.at[1, part]),
         ):
             value = flux[...].astype(jnp.float32)
-            acc[plane, at, :] = acc[plane, at, :] + value
+            acc[plane, at, :] = acc[plane, at, :] + source[plane, at, :] + value
             copy = pltpu.make_async_copy(
                 acc.at[plane, at], rate_hbm.at[plane, at], out_sem.at[which, part]
             )
@@ -521,7 +528,7 @@
         for which, plane, at, way in ((2, 1, low, 0), (3, 0, high, 1)):
             fl_copies[way, part].wait_recv()
             value = frcv[way, part].astype(jnp.float32)
-            acc[plane, at, :] = acc[plane, at, :] - value
+            acc[plane, at, :] = acc[plane, at, :] + source[plane, at, :] - value
             copy = pltpu.make_async_copy(
                 acc.at[plane, at], rate_hbm.at[plane, at], out_sem.at[which, part]
             )
@@ -532,6 +539,29 @@
     sent = x_copies + z_copies + y_copies + pr_copies + list(fl_copies.values())
     for copy in sent + [slip_up, slip_down, p_copy, r_copy, fp_copy, near_copy, tot_copy]:
         copy.wait_send()
+
+
+def hand_over(rate_in, accel_in, state_in, rate, accel, state, held, held_two, sem):
+    planes, width_y, _ = rate.shape
+    part = width_y // 4
+    ways = [(accel_in, held_two.at[0], accel), (state_in, held_two.at[1], state)]
+    for plane in range(planes):
+        for k in range(4):
+            at = (plane, pl.ds(part * k, part))
+            ways.append((rate_in.at[at], held.at[at], rate.at[at]))
+    loads = [
+        pltpu.make_async_copy(src, mid, sem.at[0, i]) for i, (src, mid, _) in enumerate(ways)
+    ]
+    stores = [
+        pltpu.make_async_copy(mid, dst, sem.at[1, i]) for i, (_, mid, dst) in enumerate(ways)
+    ]
+    for load in loads:
+        load.start()
+    for load, store in zip(loads, stores):
+        load.wait()
+        store.start()
+    for store in stores:
+        store.wait()
 
 
 def shards(
@@ -570,13 +600,14 @@
     def cut(x):
         return x.reshape(-1, 128)
 
-    rate, accel, state = pl.pallas_call(
+    shapes = (
+        jax.ShapeDtypeStruct(pressure.shape, f32),
+        jax.ShapeDtypeStruct((cells // 128, 128), f32),
+        jax.ShapeDtypeStruct((cells // 128, 128), f32),
+    )
+    results = pl.pallas_call(
         functools.partial(kernel, sizes),
-        out_shape=(
-            jax.ShapeDtypeStruct(pressure.shape, f32),
-            jax.ShapeDtypeStruct((cells // 128, 128), f32),
-            jax.ShapeDtypeStruct((cells // 128, 128), f32),
-        ),
+        out_shape=shapes,
         in_specs=[hbm] * 18,
         out_specs=(hbm, vmem, vmem),
         scratch_shapes=[
@@ -590,6 +621,7 @@
             pltpu.VMEM((planes, width_y + 2 * HALO, width_z), f32),
             pltpu.VMEM((planes, width_y + 2 * HALO, width_z), f32),
             pltpu.VMEM((planes, width_y, width_z), jnp.int32),
+            pltpu.VMEM((planes, width_y, width_z), f32),
             pltpu.VMEM((planes, width_y, width_z), f32),
             pltpu.VMEM((2, PARTS, 2, rows, width_z), bf16),
             pltpu.VMEM((2, PARTS, 2, rows, width_z), bf16),
@@ -656,6 +688,19 @@
         pressure,
         region,
     )
+    rate, accel, state = pl.pallas_call(
+        hand_over,
+        out_shape=shapes,
+        in_specs=[hbm] * 3,
+        out_specs=(hbm,) * 3,
+        scratch_shapes=[
+            pltpu.VMEM(pressure.shape, f32),
+            pltpu.VMEM((2, cells // 128, 128), f32),
+            dma((2, 10)),
+        ],
+        compiler_params=pltpu.CompilerParams(vmem_limit_bytes=60 * 1024 * 1024),
+        name="hand_over",
+    )(*results)
     return accel.reshape(cells), state.reshape(cells), rate
 
 

time: 56.3 us -> 38.9 us (0.69)
  the two profiles are of different devices: /device:TPU:1 before, /device:TPU:8 now
where the time goes in v2:
time: 38.9 us; the launch traced here: 38.7 us
  Pallas kernels  38.1 us (98%)
  between operations  0.65 us (2%)
    pallas_call x1, Pallas kernels, shards(): pl.pallas_call(functools.partial(kernel, sizes), out_shape=shapes, in_spe...  35.6 us
    pallas_call x1, Pallas kernels, shards(): pl.pallas_call(hand_over, out_shape=shapes, in_specs=[hbm] * 3, out_specs...  2.46 us

profile of v2, /device:TPU:8, one launch (start us, length us, event | category | flops | bytes accessed | tf_op | source)
XLA Modules:
  0.0 38.7 jit_solution(13835969688797578449)
XLA Ops:
  0.6 35.6 %fault_step.1 = (f32[2,256,1024]{2,1,0:T(8,128)}, f32[16,128]{1,0:T(8,128)}, f32[16,128]{1,0:T(8,128)}) custom-call(f32[16,128]{1,0:T(8,128)} %bitcast.12, f32[16,128]{1,0:T(8,128)} %bitcast.13, f32[16,128]{1,0:T(8,128)} %bitcast.14, f32[16,128]{1,0:T(8,128)} %bitcast.15, f32[16,128]{1,0:T(8,128)} %bitcast.16, f32[16,128]{1,0:T(8,128)} %bitcast.17, ...), custom_call_target="tpu_custom_call" | custom-call | tf_op jit(solution)/shard_map/fault_step/pallas_call | solution.py:608
  36.2 2.5 %hand_over.1 = (f32[2,256,1024]{2,1,0:T(8,128)}, f32[16,128]{1,0:T(8,128)}, f32[16,128]{1,0:T(8,128)}) custom-call(f32[2,256,1024]{2,1,0:T(8,128)} %get-tuple-element.9.rate_in, f32[16,128]{1,0:T(8,128)} %get-tuple-element.10.accel_in, f32[16,128]{1,0:T(8,128)} %get-tuple-element.11.state_in), custom_call_target="tpu_custom_call" | custom-call | tf_op jit(solution)/shard_map/hand_over/pallas_call | solution.py:691

commit v3 on v2

--- a/solution.py
+++ b/solution.py
@@ -86,7 +86,7 @@
     near,
     coupling,
     pick,
-    gather_x,
+    gather_xy,
     gather,
     slip_edge,
     window,
@@ -101,12 +101,10 @@
     block,
     far16,
     load_sem,
-    x_send,
-    x_recv,
+    xy_send,
+    xy_recv,
     z_send,
     z_recv,
-    y_send,
-    y_recv,
     pr_send,
     pr_recv,
     fl_send,
@@ -137,12 +135,17 @@
     above = chip_of(lax.rem(slab + 1, slabs))
     below = chip_of(lax.rem(slab + slabs - 1, slabs))
     other = (yi, zi, xi, 1 - bi)
-    x_peers = [(yi, zi, lax.rem(xi + d, nx), bi) for d in range(1, nx)]
+    xy_peers = [
+        (lax.rem(yi + dy, ny), zi, lax.rem(xi + dx, nx), bi)
+        for dy in range(ny)
+        for dx in range(nx)
+        if dy or dx
+    ]
     z_peers = [(yi, lax.rem(zi + d, nz), xi, bi) for d in range(1, nz)]
-    y_peers = [(lax.rem(yi + d, ny), zi, xi, bi) for d in range(1, ny)]
+    has_below, has_above = slab > 0, slab < slabs - 1
 
     barrier = pltpu.get_barrier_semaphore()
-    peers = [above, below, other] + x_peers + z_peers + y_peers
+    peers = [above, below, other] + xy_peers + z_peers
     for peer in peers:
         pl.semaphore_signal(barrier, inc=1, device_id=peer, device_id_type=MESH)
 
@@ -213,18 +216,18 @@
     moments = lax.dot_general(
         spread, col_basis[...], (((1,), (1,)), ((), ())), preferred_element_type=jnp.float32
     )
-    gather_x[xi] = jnp.zeros((8, 128), jnp.float32)
-    gather_x[xi, :, 0:rank] = moments
+    gather_xy[yi, xi] = jnp.zeros((8, 128), jnp.float32)
+    gather_xy[yi, xi, :, 0:rank] = moments
     for c in range(16):
         flow_row[:, 128 * c : 128 * (c + 1)] = leak[c : c + 1, :] * slip[c : c + 1, :]
 
     pl.semaphore_wait(barrier, len(peers))
 
-    x_copies = [
-        remote(gather_x.at[xi], gather_x.at[xi], x_send.at[d], x_recv.at[d], peer)
-        for d, peer in enumerate(x_peers)
+    xy_copies = [
+        remote(gather_xy.at[yi, xi], gather_xy.at[yi, xi], xy_send.at[d], xy_recv.at[d], peer)
+        for d, peer in enumerate(xy_peers)
     ]
-    for copy in x_copies:
+    for copy in xy_copies:
         copy.start()
     slip_up = remote(slip.at[8:16], slip_edge.at[0], one_send.at[0], one_recv.at[0], above)
     slip_down = remote(slip.at[0:8], slip_edge.at[1], one_send.at[1], one_recv.at[1], below)
@@ -255,9 +258,9 @@
 
     pr_copies = []
     for part in range(PARTS):
-        for way, plane, offset, device, loads in (
-            (0, 1, 0, above, first_up),
-            (1, 0, half, below, first_down),
+        for way, plane, offset, device, loads, present in (
+            (0, 1, 0, above, first_up, has_above),
+            (1, 0, half, below, first_down, has_below),
         ):
             if part == 0:
                 for copy in loads:
@@ -272,7 +275,7 @@
                 pr_recv.at[way, part],
                 device,
             )
-            copy.start()
+            pl.when(present)(copy.start)
             pr_copies.append(copy)
 
     for copy in later + tuple(behind):
@@ -327,19 +330,19 @@
     steps = cells // F_TILE
     lax.fori_loop(0, 1, sample, 0)
 
-    for copy in x_copies:
+    for copy in xy_copies:
         copy.wait_recv()
-    mine = jnp.concatenate([gather_x[i, 0:4, :] for i in range(nx)], axis=0)
-    gather[yi, zi] = mine.astype(jnp.bfloat16)
+    mine = jnp.concatenate(
+        [gather_xy[j, i, 0:4, :] for j in range(ny) for i in range(nx)], axis=0
+    )
+    gather[zi] = mine.astype(jnp.bfloat16)
     z_copies = [
-        remote(gather.at[yi, zi], gather.at[yi, zi], z_send.at[d], z_recv.at[d], peer)
+        remote(gather.at[zi], gather.at[zi], z_send.at[d], z_recv.at[d], peer)
         for d, peer in enumerate(z_peers)
     ]
     for copy in z_copies:
         copy.start()
 
-    has_below = jnp.where(slab > 0, 1.0, 0.0).astype(jnp.float32)
-    has_above = jnp.where(slab < slabs - 1, 1.0, 0.0).astype(jnp.float32)
     fl_copies = {}
 
     def faces(part):
@@ -347,13 +350,6 @@
             (0, 0, 0, below, has_below),
             (1, 1, half, above, has_above),
         ):
-            pr_copies[2 * part + way].wait_recv()
-            at = pl.ds(HALO + offset + part * rows, rows)
-            p_in = rcv[way, part, 0].astype(jnp.float32)
-            r_in = rcv[way, part, 1].astype(jnp.float32)
-            drop = pv[plane, at, :] - p_in
-            flux = drop * (inverse(rv[plane, at, :] + r_in) * -present)
-            fsnd[way, part] = flux.astype(jnp.bfloat16)
             copy = remote(
                 fsnd.at[way, part],
                 frcv.at[way, part],
@@ -361,8 +357,23 @@
                 fl_recv.at[way, part],
                 device,
             )
-            copy.start()
             fl_copies[way, part] = copy
+
+            @pl.when(present)
+            def _(way=way, plane=plane, offset=offset, copy=copy):
+                pr_copies[2 * part + way].wait_recv()
+                at = pl.ds(HALO + offset + part * rows, rows)
+                p_in = rcv[way, part, 0].astype(jnp.float32)
+                r_in = rcv[way, part, 1].astype(jnp.float32)
+                drop = p_in - pv[plane, at, :]
+                flux = drop * inverse(rv[plane, at, :] + r_in)
+                fsnd[way, part] = flux.astype(jnp.bfloat16)
+                copy.start()
+
+            @pl.when(jnp.logical_not(present))
+            def _(way=way):
+                fsnd[way, part] = jnp.zeros((rows, width_z), jnp.bfloat16)
+                frcv[1 - way, part] = jnp.zeros((rows, width_z), jnp.bfloat16)
 
     lax.fori_loop(1, 3, sample, 0)
     faces(0)
@@ -372,23 +383,12 @@
     fp_copy = remote(fp_own, fp_other, one_send.at[4], one_recv.at[4], other)
     fp_copy.start()
 
-    for copy in z_copies:
-        copy.wait_recv()
-    y_copies = [
-        remote(gather.at[yi], gather.at[yi], y_send.at[d], y_recv.at[d], peer)
-        for d, peer in enumerate(y_peers)
-    ]
-    for copy in y_copies:
-        copy.start()
-
     slip_up.wait_recv()
     slip_down.wait_recv()
-    window[0:1, :] = has_below * jnp.concatenate(
-        [slip_edge[0, 4 + q : 5 + q, :] for q in range(4)], axis=1
-    )
-    window[5:6, :] = has_above * jnp.concatenate(
-        [slip_edge[1, q : 1 + q, :] for q in range(4)], axis=1
-    )
+    edge_row = jnp.concatenate([slip_edge[0, 4 + q : 5 + q, :] for q in range(4)], axis=1)
+    window[0:1, :] = jnp.where(has_below, edge_row, 0.0)
+    edge_row = jnp.concatenate([slip_edge[1, q : 1 + q, :] for q in range(4)], axis=1)
+    window[5:6, :] = jnp.where(has_above, edge_row, 0.0)
     load_near.wait()
     for i in range(2):
         total = jnp.zeros((8, 512), jnp.float32)
@@ -445,67 +445,11 @@
         return carry
 
     spreads = width_z // Z_TILE
-    lax.fori_loop(0, spreads // 2, spread_source, 0)
+    lax.fori_loop(0, 2, spread_source, 0)
     faces(2)
+    lax.fori_loop(2, 3, spread_source, 0)
     faces(3)
-
-    for copy in last:
-        copy.wait()
-    column = lanes_row(far_col, 0, 8)
-    pick[...] = jnp.where(
-        lax.broadcasted_iota(jnp.int32, pick.shape, 0) == column, 1.0, 0.0
-    ).astype(jnp.bfloat16)
-    for copy in y_copies:
-        copy.wait_recv()
-    moments = gather[...].reshape(512, 128)[:, 0:rank]
-    picked = lax.dot_general(
-        moments, pick[...], (((0,), (0,)), ((), ())), preferred_element_type=jnp.float32
-    )
-    ranks = lanes_row(far_rank, 0, 8)
-    masked = jnp.where(
-        lax.broadcasted_iota(jnp.int32, picked.shape, 0) < ranks, picked, jnp.float32(0.0)
-    )
-    load_coupling.wait()
-    for a in range(rank):
-        block[a : a + 1, :] = jnp.sum(
-            coupling[a].astype(jnp.float32) * masked, axis=0, keepdims=True
-        )
-    target = lanes_row(far_row, 0, 8)
-    lane = lax.broadcasted_iota(jnp.int32, (rank, 128), 1)
-    totals = jnp.zeros((rank, 128), jnp.float32)
-    for c in range(4):
-        share = jnp.sum(
-            jnp.where(target == c, block[...], jnp.float32(0.0)), axis=1, keepdims=True
-        )
-        totals = totals + jnp.where(lane == c, share, jnp.float32(0.0))
-    tot_own[...] = totals
-    tot_copy = remote(tot_own, tot_other, one_send.at[6], one_recv.at[6], other)
-    tot_copy.start()
-
-    lax.fori_loop(spreads // 2, spreads, spread_source, 0)
-
-    tot_copy.wait_recv()
-    near_copy.wait_recv()
-    fp_copy.wait_recv()
-    totals = tot_own[...] + tot_other[...]
-    for c in range(4):
-        basis = row_basis[:, 512 * c : 512 * (c + 1)].astype(jnp.float32)
-        store_rows(
-            far16, 4 * c, jnp.sum(basis * totals[:, c : c + 1], axis=0, keepdims=True)
-        )
-    own, others = near_own[...], near_other[...]
-    first = bi == 0
-    near16 = jnp.concatenate(
-        [jnp.where(first, own, others), jnp.where(first, others, own)], axis=0
-    )
-    traction = near16 + far16[...]
-    effective = stress[...] - (fp_own[...] + fp_other[...])
-    rate = slip[...]
-    state_rate = jnp.exp(-log_state[...]) - rate
-    accel_out[...] = (traction - effective * friction_b[...] * state_rate) / (
-        effective * friction_a[...] / rate + 0.5
-    )
-    state_out[...] = state_rate
+    lax.fori_loop(3, spreads, spread_source, 0)
 
     stores = []
     for part in range(PARTS):
@@ -522,11 +466,52 @@
             )
             copy.start()
             stores.append(copy)
+
+    for copy in last:
+        copy.wait()
+    column = lanes_row(far_col, 0, 8)
+    group = nx * 4
+    column = (
+        ((column // group) % nz) * (ny * group) + (column // (nz * group)) * group + column % group
+    )
+    pick[...] = jnp.where(
+        lax.broadcasted_iota(jnp.int32, pick.shape, 0) == column, 1.0, 0.0
+    ).astype(jnp.bfloat16)
+    for copy in z_copies:
+        copy.wait_recv()
+    moments = gather[...].reshape(512, 128)[:, 0:rank]
+    picked = lax.dot_general(
+        moments, pick[...], (((0,), (0,)), ((), ())), preferred_element_type=jnp.float32
+    )
+    ranks = lanes_row(far_rank, 0, 8)
+    masked = jnp.where(
+        lax.broadcasted_iota(jnp.int32, picked.shape, 0) < ranks, picked, jnp.float32(0.0)
+    )
+    load_coupling.wait()
+    for a in range(rank):
+        block[a : a + 1, :] = jnp.sum(
+            coupling[a].astype(jnp.float32) * masked, axis=0, keepdims=True
+        )
+    target = lanes_row(far_row, 0, 8)
+    lane = lax.broadcasted_iota(jnp.int32, (rank, 128), 1)
+    totals = jnp.zeros((rank, 128), jnp.float32)
+    for c in range(4):
+        share = jnp.sum(
+            jnp.where(target == c, block[...], jnp.float32(0.0)), axis=1, keepdims=True
+        )
+        totals = totals + jnp.where(lane == c, share, jnp.float32(0.0))
+    tot_own[...] = totals
+    tot_copy = remote(tot_own, tot_other, one_send.at[6], one_recv.at[6], other)
+    tot_copy.start()
+
     for part in range(PARTS):
         low = pl.ds(part * rows, rows)
         high = pl.ds(half + part * rows, rows)
-        for which, plane, at, way in ((2, 1, low, 0), (3, 0, high, 1)):
-            fl_copies[way, part].wait_recv()
+        for which, plane, at, way, present in (
+            (2, 1, low, 0, has_above),
+            (3, 0, high, 1, has_below),
+        ):
+            pl.when(present)(fl_copies[way, part].wait_recv)
             value = frcv[way, part].astype(jnp.float32)
             acc[plane, at, :] = acc[plane, at, :] + source[plane, at, :] - value
             copy = pltpu.make_async_copy(
@@ -534,10 +519,37 @@
             )
             copy.start()
             stores.append(copy)
+
+    tot_copy.wait_recv()
+    near_copy.wait_recv()
+    fp_copy.wait_recv()
+    totals = tot_own[...] + tot_other[...]
+    for c in range(4):
+        basis = row_basis[:, 512 * c : 512 * (c + 1)].astype(jnp.float32)
+        store_rows(
+            far16, 4 * c, jnp.sum(basis * totals[:, c : c + 1], axis=0, keepdims=True)
+        )
+    own, others = near_own[...], near_other[...]
+    first = bi == 0
+    near16 = jnp.concatenate(
+        [jnp.where(first, own, others), jnp.where(first, others, own)], axis=0
+    )
+    traction = near16 + far16[...]
+    effective = stress[...] - (fp_own[...] + fp_other[...])
+    rate = slip[...]
+    state_rate = jnp.exp(-log_state[...]) - rate
+    accel_out[...] = (traction - effective * friction_b[...] * state_rate) / (
+        effective * friction_a[...] / rate + 0.5
+    )
+    state_out[...] = state_rate
+
     for copy in stores:
         copy.wait()
-    sent = x_copies + z_copies + y_copies + pr_copies + list(fl_copies.values())
-    for copy in sent + [slip_up, slip_down, p_copy, r_copy, fp_copy, near_copy, tot_copy]:
+    for part in range(PARTS):
+        for way, there, back in ((0, has_above, has_below), (1, has_below, has_above)):
+            pl.when(there)(pr_copies[2 * part + way].wait_send)
+            pl.when(back)(fl_copies[way, part].wait_send)
+    for copy in xy_copies + z_copies + [slip_up, slip_down, p_copy, r_copy, fp_copy, near_copy, tot_copy]:
         copy.wait_send()
 
 
@@ -635,8 +647,8 @@
             pltpu.VMEM(near_blocks.shape, bf16),
             pltpu.VMEM(far_coupling.shape, bf16),
             pltpu.VMEM((ny * nz * nx * clusters, slots), bf16),
-            pltpu.VMEM((nx, 8, 128), f32),
-            pltpu.VMEM((ny, nz, nx * clusters, 128), bf16),
+            pltpu.VMEM((ny, nx, 8, 128), f32),
+            pltpu.VMEM((nz, ny * nx * clusters, 128), bf16),
             pltpu.VMEM((2, 8, 128), f32),
             pltpu.VMEM((8, 512), f32),
             pltpu.VMEM((1, cells), f32),
@@ -650,12 +662,10 @@
             pltpu.VMEM((rank, slots), f32),
             pltpu.VMEM((cells // 128, 128), f32),
             dma((24,)),
-            dma((nx - 1,)),
-            dma((nx - 1,)),
+            dma((ny * nx - 1,)),
+            dma((ny * nx - 1,)),
             dma((nz - 1,)),
             dma((nz - 1,)),
-            dma((ny - 1,)),
-            dma((ny - 1,)),
             dma((2, PARTS)),
             dma((2, PARTS)),
             dma((2, PARTS)),

time: 38.9 us -> 42.9 us (1.10)
  Pallas kernels: 38.1 us -> 42.1 us
    pallas_call x1, Pallas kernels: 35.6 us -> 39.6 us  [shards(): pl.pallas_call(functools.partial(kernel, sizes), out_shape=shapes, in_spe...]
where the time goes in v3:
time: 42.9 us; the launch traced here: 42.7 us
  Pallas kernels  42.1 us (98%)
  between operations  0.65 us (2%)
    pallas_call x1, Pallas kernels, shards(): pl.pallas_call(functools.partial(kernel, sizes), out_shape=shapes, in_spe...  39.6 us
    pallas_call x1, Pallas kernels, shards(): pl.pallas_call(hand_over, out_shape=shapes, in_specs=[hbm] * 3, out_specs...  2.46 us

profile of v3, /device:TPU:8, one launch (start us, length us, event | category | flops | bytes accessed | tf_op | source)
XLA Modules:
  0.0 42.7 jit_solution(14226604875663285866)
XLA Ops:
  0.6 39.6 %fault_step.1 = (f32[2,256,1024]{2,1,0:T(8,128)}, f32[16,128]{1,0:T(8,128)}, f32[16,128]{1,0:T(8,128)}) custom-call(f32[16,128]{1,0:T(8,128)} %bitcast.12, f32[16,128]{1,0:T(8,128)} %bitcast.13, f32[16,128]{1,0:T(8,128)} %bitcast.14, f32[16,128]{1,0:T(8,128)} %bitcast.15, f32[16,128]{1,0:T(8,128)} %bitcast.16, f32[16,128]{1,0:T(8,128)} %bitcast.17, ...), custom_call_target="tpu_custom_call" | custom-call | tf_op jit(solution)/shard_map/fault_step/pallas_call | solution.py:620
  40.2 2.5 %hand_over.1 = (f32[2,256,1024]{2,1,0:T(8,128)}, f32[16,128]{1,0:T(8,128)}, f32[16,128]{1,0:T(8,128)}) custom-call(f32[2,256,1024]{2,1,0:T(8,128)} %get-tuple-element.9.rate_in, f32[16,128]{1,0:T(8,128)} %get-tuple-element.10.accel_in, f32[16,128]{1,0:T(8,128)} %get-tuple-element.11.state_in), custom_call_target="tpu_custom_call" | custom-call | tf_op jit(solution)/shard_map/hand_over/pallas_call | solution.py:701

commit v4 on v3

--- a/solution.py
+++ b/solution.py
@@ -86,7 +86,7 @@
     near,
     coupling,
     pick,
-    gather_xy,
+    gather_x,
     gather,
     slip_edge,
     window,
@@ -101,10 +101,12 @@
     block,
     far16,
     load_sem,
-    xy_send,
-    xy_recv,
+    x_send,
+    x_recv,
     z_send,
     z_recv,
+    y_send,
+    y_recv,
     pr_send,
     pr_recv,
     fl_send,
@@ -135,17 +137,13 @@
     above = chip_of(lax.rem(slab + 1, slabs))
     below = chip_of(lax.rem(slab + slabs - 1, slabs))
     other = (yi, zi, xi, 1 - bi)
-    xy_peers = [
-        (lax.rem(yi + dy, ny), zi, lax.rem(xi + dx, nx), bi)
-        for dy in range(ny)
-        for dx in range(nx)
-        if dy or dx
-    ]
+    x_peers = [(yi, zi, lax.rem(xi + d, nx), bi) for d in range(1, nx)]
+    y_peers = [(lax.rem(yi + d, ny), zi, xi, bi) for d in range(1, ny)]
     z_peers = [(yi, lax.rem(zi + d, nz), xi, bi) for d in range(1, nz)]
     has_below, has_above = slab > 0, slab < slabs - 1
 
     barrier = pltpu.get_barrier_semaphore()
-    peers = [above, below, other] + xy_peers + z_peers
+    peers = [above, below, other] + x_peers + z_peers + y_peers
     for peer in peers:
         pl.semaphore_signal(barrier, inc=1, device_id=peer, device_id_type=MESH)
 
@@ -199,8 +197,6 @@
     last = small[6:]
     for copy in ahead[:3] + list(first_up + first_down) + ahead[3:] + behind + list(later):
         copy.start()
-    for copy in [load_near, load_coupling] + last:
-        copy.start()
     for copy in ahead:
         copy.wait()
 
@@ -216,18 +212,18 @@
     moments = lax.dot_general(
         spread, col_basis[...], (((1,), (1,)), ((), ())), preferred_element_type=jnp.float32
     )
-    gather_xy[yi, xi] = jnp.zeros((8, 128), jnp.float32)
-    gather_xy[yi, xi, :, 0:rank] = moments
+    gather_x[xi] = jnp.zeros((8, 128), jnp.float32)
+    gather_x[xi, :, 0:rank] = moments
     for c in range(16):
         flow_row[:, 128 * c : 128 * (c + 1)] = leak[c : c + 1, :] * slip[c : c + 1, :]
 
     pl.semaphore_wait(barrier, len(peers))
 
-    xy_copies = [
-        remote(gather_xy.at[yi, xi], gather_xy.at[yi, xi], xy_send.at[d], xy_recv.at[d], peer)
-        for d, peer in enumerate(xy_peers)
+    x_copies = [
+        remote(gather_x.at[xi], gather_x.at[xi], x_send.at[d], x_recv.at[d], peer)
+        for d, peer in enumerate(x_peers)
     ]
-    for copy in xy_copies:
+    for copy in x_copies:
         copy.start()
     slip_up = remote(slip.at[8:16], slip_edge.at[0], one_send.at[0], one_recv.at[0], above)
     slip_down = remote(slip.at[0:8], slip_edge.at[1], one_send.at[1], one_recv.at[1], below)
@@ -275,9 +271,12 @@
                 pr_recv.at[way, part],
                 device,
             )
-            pl.when(present)(copy.start)
+            if part < PARTS - 1:
+                pl.when(present)(copy.start)
             pr_copies.append(copy)
 
+    for copy in [load_near, load_coupling] + last:
+        copy.start()
     for copy in later + tuple(behind):
         copy.wait()
 
@@ -329,15 +328,17 @@
 
     steps = cells // F_TILE
     lax.fori_loop(0, 1, sample, 0)
-
-    for copy in xy_copies:
+    pl.when(has_above)(pr_copies[2 * PARTS - 2].start)
+    pl.when(has_below)(pr_copies[2 * PARTS - 1].start)
+
+    for copy in x_copies:
         copy.wait_recv()
     mine = jnp.concatenate(
-        [gather_xy[j, i, 0:4, :] for j in range(ny) for i in range(nx)], axis=0
-    )
-    gather[zi] = mine.astype(jnp.bfloat16)
+        [gather_x[i, 0:4, :] for i in range(nx)], axis=0
+    )
+    gather[yi, zi] = mine.astype(jnp.bfloat16)
     z_copies = [
-        remote(gather.at[zi], gather.at[zi], z_send.at[d], z_recv.at[d], peer)
+        remote(gather.at[yi, zi], gather.at[yi, zi], z_send.at[d], z_recv.at[d], peer)
         for d, peer in enumerate(z_peers)
     ]
     for copy in z_copies:
@@ -382,6 +383,15 @@
         fp_own[c : c + 1, :] = fp_row[:, 128 * c : 128 * (c + 1)]
     fp_copy = remote(fp_own, fp_other, one_send.at[4], one_recv.at[4], other)
     fp_copy.start()
+
+    for copy in z_copies:
+        copy.wait_recv()
+    y_copies = [
+        remote(gather.at[yi], gather.at[yi], y_send.at[d], y_recv.at[d], peer)
+        for d, peer in enumerate(y_peers)
+    ]
+    for copy in y_copies:
+        copy.start()
 
     slip_up.wait_recv()
     slip_down.wait_recv()
@@ -449,6 +459,39 @@
     faces(2)
     lax.fori_loop(2, 3, spread_source, 0)
     faces(3)
+    for copy in last:
+        copy.wait()
+    column = lanes_row(far_col, 0, 8)
+    pick[...] = jnp.where(
+        lax.broadcasted_iota(jnp.int32, pick.shape, 0) == column, 1.0, 0.0
+    ).astype(jnp.bfloat16)
+    for copy in y_copies:
+        copy.wait_recv()
+    moments = gather[...].reshape(512, 128)[:, 0:rank]
+    picked = lax.dot_general(
+        moments, pick[...], (((0,), (0,)), ((), ())), preferred_element_type=jnp.float32
+    )
+    ranks = lanes_row(far_rank, 0, 8)
+    masked = jnp.where(
+        lax.broadcasted_iota(jnp.int32, picked.shape, 0) < ranks, picked, jnp.float32(0.0)
+    )
+    load_coupling.wait()
+    for a in range(rank):
+        block[a : a + 1, :] = jnp.sum(
+            coupling[a].astype(jnp.float32) * masked, axis=0, keepdims=True
+        )
+    target = lanes_row(far_row, 0, 8)
+    lane = lax.broadcasted_iota(jnp.int32, (rank, 128), 1)
+    totals = jnp.zeros((rank, 128), jnp.float32)
+    for c in range(4):
+        share = jnp.sum(
+            jnp.where(target == c, block[...], jnp.float32(0.0)), axis=1, keepdims=True
+        )
+        totals = totals + jnp.where(lane == c, share, jnp.float32(0.0))
+    tot_own[...] = totals
+    tot_copy = remote(tot_own, tot_other, one_send.at[6], one_recv.at[6], other)
+    tot_copy.start()
+
     lax.fori_loop(3, spreads, spread_source, 0)
 
     stores = []
@@ -467,43 +510,6 @@
             copy.start()
             stores.append(copy)
 
-    for copy in last:
-        copy.wait()
-    column = lanes_row(far_col, 0, 8)
-    group = nx * 4
-    column = (
-        ((column // group) % nz) * (ny * group) + (column // (nz * group)) * group + column % group
-    )
-    pick[...] = jnp.where(
-        lax.broadcasted_iota(jnp.int32, pick.shape, 0) == column, 1.0, 0.0
-    ).astype(jnp.bfloat16)
-    for copy in z_copies:
-        copy.wait_recv()
-    moments = gather[...].reshape(512, 128)[:, 0:rank]
-    picked = lax.dot_general(
-        moments, pick[...], (((0,), (0,)), ((), ())), preferred_element_type=jnp.float32
-    )
-    ranks = lanes_row(far_rank, 0, 8)
-    masked = jnp.where(
-        lax.broadcasted_iota(jnp.int32, picked.shape, 0) < ranks, picked, jnp.float32(0.0)
-    )
-    load_coupling.wait()
-    for a in range(rank):
-        block[a : a + 1, :] = jnp.sum(
-            coupling[a].astype(jnp.float32) * masked, axis=0, keepdims=True
-        )
-    target = lanes_row(far_row, 0, 8)
-    lane = lax.broadcasted_iota(jnp.int32, (rank, 128), 1)
-    totals = jnp.zeros((rank, 128), jnp.float32)
-    for c in range(4):
-        share = jnp.sum(
-            jnp.where(target == c, block[...], jnp.float32(0.0)), axis=1, keepdims=True
-        )
-        totals = totals + jnp.where(lane == c, share, jnp.float32(0.0))
-    tot_own[...] = totals
-    tot_copy = remote(tot_own, tot_other, one_send.at[6], one_recv.at[6], other)
-    tot_copy.start()
-
     for part in range(PARTS):
         low = pl.ds(part * rows, rows)
         high = pl.ds(half + part * rows, rows)
@@ -549,7 +555,7 @@
         for way, there, back in ((0, has_above, has_below), (1, has_below, has_above)):
             pl.when(there)(pr_copies[2 * part + way].wait_send)
             pl.when(back)(fl_copies[way, part].wait_send)
-    for copy in xy_copies + z_copies + [slip_up, slip_down, p_copy, r_copy, fp_copy, near_copy, tot_copy]:
+    for copy in x_copies + z_copies + y_copies + [slip_up, slip_down, p_copy, r_copy, fp_copy, near_copy, tot_copy]:
         copy.wait_send()
 
 
@@ -647,8 +653,8 @@
             pltpu.VMEM(near_blocks.shape, bf16),
             pltpu.VMEM(far_coupling.shape, bf16),
             pltpu.VMEM((ny * nz * nx * clusters, slots), bf16),
-            pltpu.VMEM((ny, nx, 8, 128), f32),
-            pltpu.VMEM((nz, ny * nx * clusters, 128), bf16),
+            pltpu.VMEM((nx, 8, 128), f32),
+            pltpu.VMEM((ny, nz, nx * clusters, 128), bf16),
             pltpu.VMEM((2, 8, 128), f32),
             pltpu.VMEM((8, 512), f32),
             pltpu.VMEM((1, cells), f32),
@@ -662,10 +668,12 @@
             pltpu.VMEM((rank, slots), f32),
             pltpu.VMEM((cells // 128, 128), f32),
             dma((24,)),
-            dma((ny * nx - 1,)),
-            dma((ny * nx - 1,)),
+            dma((nx - 1,)),
+            dma((nx - 1,)),
             dma((nz - 1,)),
             dma((nz - 1,)),
+            dma((ny - 1,)),
+            dma((ny - 1,)),
             dma((2, PARTS)),
             dma((2, PARTS)),
             dma((2, PARTS)),

time: 42.9 us -> 39.6 us (0.923)
  Pallas kernels: 42.1 us -> 38.7 us
    pallas_call x1, Pallas kernels: 39.6 us -> 36.2 us  [shards(): pl.pallas_call(functools.partial(kernel, sizes), out_shape=shapes, in_spe...]
where the time goes in v4:
time: 39.6 us; the launch traced here: 39.4 us
  Pallas kernels  38.7 us (98%)
  between operations  0.65 us (2%)
    pallas_call x1, Pallas kernels, shards(): pl.pallas_call(functools.partial(kernel, sizes), out_shape=shapes, in_spe...  36.2 us
    pallas_call x1, Pallas kernels, shards(): pl.pallas_call(hand_over, out_shape=shapes, in_specs=[hbm] * 3, out_specs...  2.46 us

profile of v4, /device:TPU:8, one launch (start us, length us, event | category | flops | bytes accessed | tf_op | source)
XLA Modules:
  0.0 39.4 jit_solution(14074398607927340761)
XLA Ops:
  0.6 36.2 %fault_step.1 = (f32[2,256,1024]{2,1,0:T(8,128)}, f32[16,128]{1,0:T(8,128)}, f32[16,128]{1,0:T(8,128)}) custom-call(f32[16,128]{1,0:T(8,128)} %bitcast.12, f32[16,128]{1,0:T(8,128)} %bitcast.13, f32[16,128]{1,0:T(8,128)} %bitcast.14, f32[16,128]{1,0:T(8,128)} %bitcast.15, f32[16,128]{1,0:T(8,128)} %bitcast.16, f32[16,128]{1,0:T(8,128)} %bitcast.17, ...), custom_call_target="tpu_custom_call" | custom-call | tf_op jit(solution)/shard_map/fault_step/pallas_call | solution.py:626
  36.9 2.5 %hand_over.1 = (f32[2,256,1024]{2,1,0:T(8,128)}, f32[16,128]{1,0:T(8,128)}, f32[16,128]{1,0:T(8,128)}) custom-call(f32[2,256,1024]{2,1,0:T(8,128)} %get-tuple-element.9.rate_in, f32[16,128]{1,0:T(8,128)} %get-tuple-element.10.accel_in, f32[16,128]{1,0:T(8,128)} %get-tuple-element.11.state_in), custom_call_target="tpu_custom_call" | custom-call | tf_op jit(solution)/shard_map/hand_over/pallas_call | solution.py:709

commit v5 on v2

--- a/solution.py
+++ b/solution.py
@@ -484,29 +484,6 @@
 
     lax.fori_loop(spreads // 2, spreads, spread_source, 0)
 
-    tot_copy.wait_recv()
-    near_copy.wait_recv()
-    fp_copy.wait_recv()
-    totals = tot_own[...] + tot_other[...]
-    for c in range(4):
-        basis = row_basis[:, 512 * c : 512 * (c + 1)].astype(jnp.float32)
-        store_rows(
-            far16, 4 * c, jnp.sum(basis * totals[:, c : c + 1], axis=0, keepdims=True)
-        )
-    own, others = near_own[...], near_other[...]
-    first = bi == 0
-    near16 = jnp.concatenate(
-        [jnp.where(first, own, others), jnp.where(first, others, own)], axis=0
-    )
-    traction = near16 + far16[...]
-    effective = stress[...] - (fp_own[...] + fp_other[...])
-    rate = slip[...]
-    state_rate = jnp.exp(-log_state[...]) - rate
-    accel_out[...] = (traction - effective * friction_b[...] * state_rate) / (
-        effective * friction_a[...] / rate + 0.5
-    )
-    state_out[...] = state_rate
-
     stores = []
     for part in range(PARTS):
         low = pl.ds(part * rows, rows)
@@ -522,6 +499,30 @@
             )
             copy.start()
             stores.append(copy)
+
+    tot_copy.wait_recv()
+    near_copy.wait_recv()
+    fp_copy.wait_recv()
+    totals = tot_own[...] + tot_other[...]
+    for c in range(4):
+        basis = row_basis[:, 512 * c : 512 * (c + 1)].astype(jnp.float32)
+        store_rows(
+            far16, 4 * c, jnp.sum(basis * totals[:, c : c + 1], axis=0, keepdims=True)
+        )
+    own, others = near_own[...], near_other[...]
+    first = bi == 0
+    near16 = jnp.concatenate(
+        [jnp.where(first, own, others), jnp.where(first, others, own)], axis=0
+    )
+    traction = near16 + far16[...]
+    effective = stress[...] - (fp_own[...] + fp_other[...])
+    rate = slip[...]
+    state_rate = jnp.exp(-log_state[...]) - rate
+    accel_out[...] = (traction - effective * friction_b[...] * state_rate) / (
+        effective * friction_a[...] / rate + 0.5
+    )
+    state_out[...] = state_rate
+
     for part in range(PARTS):
         low = pl.ds(part * rows, rows)
         high = pl.ds(half + part * rows, rows)

time: 38.9 us -> 38.9 us (level)
  no operation moved by 1% of the time
where the time goes in v5:
time: 38.9 us; the launch traced here: 38.7 us
  Pallas kernels  38.1 us (98%)
  between operations  0.65 us (2%)
    pallas_call x1, Pallas kernels, shards(): pl.pallas_call(functools.partial(kernel, sizes), out_shape=shapes, in_spe...  35.6 us
    pallas_call x1, Pallas kernels, shards(): pl.pallas_call(hand_over, out_shape=shapes, in_specs=[hbm] * 3, out_specs...  2.46 us

profile of v5, /device:TPU:8, one launch (start us, length us, event | category | flops | bytes accessed | tf_op | source)
XLA Modules:
  0.0 38.7 jit_solution(518708455370731095)
XLA Ops:
  0.6 35.6 %fault_step.1 = (f32[2,256,1024]{2,1,0:T(8,128)}, f32[16,128]{1,0:T(8,128)}, f32[16,128]{1,0:T(8,128)}) custom-call(f32[16,128]{1,0:T(8,128)} %bitcast.12, f32[16,128]{1,0:T(8,128)} %bitcast.13, f32[16,128]{1,0:T(8,128)} %bitcast.14, f32[16,128]{1,0:T(8,128)} %bitcast.15, f32[16,128]{1,0:T(8,128)} %bitcast.16, f32[16,128]{1,0:T(8,128)} %bitcast.17, ...), custom_call_target="tpu_custom_call" | custom-call | tf_op jit(solution)/shard_map/fault_step/pallas_call | solution.py:609
  36.2 2.5 %hand_over.1 = (f32[2,256,1024]{2,1,0:T(8,128)}, f32[16,128]{1,0:T(8,128)}, f32[16,128]{1,0:T(8,128)}) custom-call(f32[2,256,1024]{2,1,0:T(8,128)} %get-tuple-element.9.rate_in, f32[16,128]{1,0:T(8,128)} %get-tuple-element.10.accel_in, f32[16,128]{1,0:T(8,128)} %get-tuple-element.11.state_in), custom_call_target="tpu_custom_call" | custom-call | tf_op jit(solution)/shard_map/hand_over/pallas_call | solution.py:692
